TPU v7x, 32 devices: a whole 2x2x4 slice. The times are simulated.
32 devices in a mesh: ctx: 8 (over z, x), head: 4 (over y, core).
Axes of the slice: x: 2, y: 2, z: 4, core: 2. Of those that a mesh axis runs over, the one named last changes fastest.
Arguments:
- queries: bfloat16 [1024, 2048], P('ctx', 'head'), may hold values from -120 to 120
- keys: bfloat16 [1024, 512], P('ctx', 'head'), may hold values from -4.5 to 4.5
- values: bfloat16 [1024, 512], P('ctx', 'head'), may hold values from -6 to 6
- segments: int32 [1024], replicated, may hold values from 0 to 2, never falling along the last dimension, each value on 1 to 512 neighbouring positions
- residual: bfloat16 [1024, 8192], P('ctx', 'head'), may hold values from -1.5 to 1.5
- out_weight: bfloat16 [2048, 8192], P('head'), may hold values from -1.5 to 1.5
Outputs:
- mixed: bfloat16 [1024, 8192], P('ctx', 'head')
Inputs may be any that keep to these rules, and one draw needn't show every extreme that they name: `segments`: no document is longer than 512 positions.
All inputs are finite; a program needn't handle non-finite values.
Results may differ from a plain program's by a relative error of at most 0.015.
Values may be sent and summed in bfloat16 or wider, within the bound.
A program may use at most 128 MiB of HBM per device.

v0:
```python
import math

import jax
import jax.numpy as jnp
from jax import lax
from jax.sharding import PartitionSpec as P

HD = 128


def passed_along(x, axis, by):
    peers = lax.axis_size(axis)
    pairs = [(i, i + by) for i in range(peers) if 0 <= i + by < peers]
    return lax.ppermute(x, axis, pairs)


def local(queries, keys, values, segments, residual, out_weight):
    tok_rows = queries.shape[0]
    group_size = queries.shape[1] // HD
    ctx_count = lax.axis_size("ctx")
    ctx_index = lax.axis_index("ctx")
    query_first = ctx_index * tok_rows
    score_scale = 1.0 / math.sqrt(HD)
    query_rows = (
        queries.reshape(tok_rows, group_size, HD)
        .transpose(1, 0, 2)
        .reshape(group_size * tok_rows, HD)
    )
    query_segment = lax.dynamic_slice_in_dim(segments, query_first, tok_rows, 0)
    query_position = query_first + jnp.arange(tok_rows, dtype=jnp.int32)
    history_rows = tok_rows * ctx_count
    padded_segment = jnp.concatenate([jnp.full((history_rows,), -1, jnp.int32), segments])
    start_state = (
        jnp.full((group_size * tok_rows,), -1e30, jnp.float32),
        jnp.zeros((group_size * tok_rows,), jnp.float32),
        jnp.zeros((group_size * tok_rows, HD), jnp.float32),
    )
    farthest = ctx_count // 2
    doubling_count = farthest.bit_length()
    buffered = jnp.concatenate([keys, values], axis=1)
    for bit_number in range(doubling_count):
        earlier = passed_along(buffered, "ctx", 1 << bit_number)
        buffered = jnp.concatenate([earlier, buffered], axis=0)
    buffer_rows = buffered.shape[0]
    buffer_first = (ctx_index - ((1 << doubling_count) - 1)) * tok_rows
    running = start_state
    block_span = max(tok_rows, 2048)
    for offset in range(0, buffer_rows, block_span):
        width_here = min(block_span, buffer_rows - offset)
        block_kv = buffered[offset : offset + width_here]
        first_row = buffer_first + offset
        key_block = block_kv[:, :HD]
        value_block = block_kv[:, HD:]
        count_rows = key_block.shape[0]
        key_segment = lax.dynamic_slice_in_dim(
            padded_segment, first_row + history_rows, count_rows, 0
        )
        key_position = first_row + jnp.arange(count_rows, dtype=jnp.int32)
        visible = (query_segment[:, None] == key_segment[None, :]) & (
            key_position[None, :] <= query_position[:, None]
        )
        visible = jnp.tile(visible, (group_size, 1))
        scores = (
            lax.dot_general(
                query_rows, key_block, (((1,), (1,)), ((), ())), preferred_element_type=jnp.float32
            )
            * score_scale
        )
        scores = jnp.where(visible, scores, -jnp.inf)
        best_old, total_old, summed_old = running
        best_new = jnp.maximum(best_old, jnp.max(scores, axis=1))
        shrink = jnp.exp(best_old - best_new)
        raw_weights = jnp.exp(scores - best_new[:, None])
        total_new = total_old * shrink + jnp.sum(raw_weights, axis=1)
        summed_new = summed_old * shrink[:, None] + jnp.dot(
            raw_weights.astype(jnp.bfloat16), value_block, preferred_element_type=jnp.float32
        )
        running = (best_new, total_new, summed_new)
    best_row, total_row, summed_row = running
    attended = (summed_row / total_row[:, None]).astype(jnp.bfloat16)
    attended = (
        attended.reshape(group_size, tok_rows, HD)
        .transpose(1, 0, 2)
        .reshape(tok_rows, group_size * HD)
    )
    partial_out = jnp.dot(attended, out_weight, preferred_element_type=jnp.float32)
    summed_out = lax.psum_scatter(
        partial_out.astype(jnp.bfloat16), "head", scatter_dimension=1, tiled=True
    ).astype(jnp.float32)
    return (residual.astype(jnp.float32) + summed_out).astype(jnp.bfloat16)


def solution(mesh):
    placed = (
        P("ctx", "head"),
        P("ctx", "head"),
        P("ctx", "head"),
        P(),
        P("ctx", "head"),
        P("head", None),
    )
    return jax.shard_map(
        local, mesh=mesh, in_specs=placed, out_specs=P("ctx", "head"), check_vma=False
    )
```

profile of v0, /device:TPU:0, one launch (start us, length us, event | category | flops | bytes accessed | tf_op | source)
XLA Modules:
  0.0 86.5 jit_solution(15681202298284877345)
XLA Ops:
  6.5 0.0 reduce-scatter.2.cloned.1.call-start
  6.5 0.8 constant_dynamic-update-slice_fusion.1
  7.3 0.8 constant_dynamic-update-slice_fusion
  8.1 4.8 %collective-permute-start = (bf16[128,256]{1,0:T(8,128)(2,1)S(1)}, bf16[128,256]{1,0:T(8,128)(2,1)S(1)}, u32[]{:S(2)}, u32[]{:S(2)}) collective-permute-start(bf16[128,256]{1,0:T(8,128)(2,1)S(1)} %constant_dynamic-update-slice_fusion), channel_id=1, source_target_pairs={{0,4},{4,8},{8,12},{12,16},{16,20},{20,24},{24,28},{1,5},{5,9},{9,... | collective-permute-start | bytes 196616 | tf_op jit(solution)/shard_map/ppermute | solution.py:14
  12.9 1.9 %collective-permute-done = bf16[128,256]{1,0:T(8,128)(2,1)S(1)} collective-permute-done((bf16[128,256]{1,0:T(8,128)(2,1)S(1)}, bf16[128,256]{1,0:T(8,128)(2,1)S(1)}, u32[]{:S(2)}, u32[]{:S(2)}) %collective-permute-start) | collective-permute-done | bytes 65568 | tf_op jit(solution)/shard_map/ppermute | solution.py:14
  14.8 5.3 %collective-permute-start.1 = (bf16[256,256]{1,0:T(8,128)(2,1)S(1)}, bf16[256,256]{1,0:T(8,128)(2,1)S(1)}, u32[]{:S(2)}, u32[]{:S(2)}) collective-permute-start(bf16[256,256]{1,0:T(8,128)(2,1)S(1)} %pad_maximum_fusion.2), channel_id=1, source_target_pairs={{0,8},{4,12},{8,16},{12,20},{16,24},{20,28},{1,9},{5,13},{9,17},{1... | collective-permute-start | bytes 393224 | tf_op jit(solution)/shard_map/ppermute | solution.py:14
  20.1 0.8 pad_dynamic-slice_fusion
  20.9 1.7 %collective-permute-done.1 = bf16[256,256]{1,0:T(8,128)(2,1)S(1)} collective-permute-done((bf16[256,256]{1,0:T(8,128)(2,1)S(1)}, bf16[256,256]{1,0:T(8,128)(2,1)S(1)}, u32[]{:S(2)}, u32[]{:S(2)}) %collective-permute-start.1) | collective-permute-done | bytes 131104 | tf_op jit(solution)/shard_map/ppermute | solution.py:14
  22.6 5.4 %collective-permute-start.2 = (bf16[512,256]{1,0:T(8,128)(2,1)S(1)}, bf16[512,256]{1,0:T(8,128)(2,1)S(1)}, u32[]{:S(2)}, u32[]{:S(2)}) collective-permute-start(bf16[512,256]{1,0:T(8,128)(2,1)S(1)} %pad_maximum_fusion.1), channel_id=1, source_target_pairs={{0,16},{4,20},{8,24},{12,28},{1,17},{5,21},{9,25},{13,29},{2,18},{... | collective-permute-start | bytes 786440 | tf_op jit(solution)/shard_map/ppermute | solution.py:14
  28.0 0.8 dynamic_slice.6
  28.8 1.0 %copy.8 = bf16[128,512]{0,1:T(8,128)(2,1)S(1)} copy(bf16[128,512]{1,0:T(8,128)(2,1)} %param.6) | data formatting | bytes 262144 | tf_op args[0]
  29.8 0.1 copy.9
  29.9 0.3 compare_and_fusion
  30.3 1.6 %collective-permute-done.2 = bf16[512,256]{1,0:T(8,128)(2,1)S(1)} collective-permute-done((bf16[512,256]{1,0:T(8,128)(2,1)S(1)}, bf16[512,256]{1,0:T(8,128)(2,1)S(1)}, u32[]{:S(2)}, u32[]{:S(2)}) %collective-permute-start.2) | collective-permute-done | bytes 262176 | tf_op jit(solution)/shard_map/ppermute | solution.py:14
  31.9 0.5 tile.4
  32.4 0.6 fusion.9
  33.0 0.4 fusion
  33.4 0.5 fusion.3
  33.9 0.1 copy.10
  34.0 6.0 %convolution_convert_fusion = bf16[128,8192]{1,0:T(8,128)(2,1)} fusion(bf16[128,512]{0,1:T(8,128)(2,1)S(1)} %bitcast.20, bf16[512,8192]{1,0:T(8,128)(2,1)} %param.11), kind=kOutput, calls=%fused_computation | convolution fusion | flops 1074790400 | bytes 10616832 | tf_op jit(solution)/shard_map/dot_general | solution.py:86
  40.1 0.0 copy-start
  40.1 0.0 reduce-scatter.2.cloned.1.call-update
  40.1 37.6 %reduce-scatter.2.cloned.1.call-done = bf16[128,2048]{1,0:T(8,128)(2,1)} async-done(((bf16[128,8192]{1,0:T(8,128)(2,1)}), bf16[128,2048]{1,0:T(8,128)(2,1)}) %reduce-scatter.2.cloned.1.call-update) | async-done | bytes 524304 | tf_op jit(solution)/shard_map/reduce_scatter | solution.py:87
  77.7 0.0 copy-done
  77.7 2.0 %add_convert_fusion = bf16[128,2048]{1,0:T(8,128)(2,1)} fusion(bf16[128,2048]{1,0:T(8,128)(2,1)} %reduce-scatter.2.cloned.1.call-done, bf16[128,2048]{1,0:T(8,128)(2,1)S(1)} %copy-done), kind=kLoop, calls=%fused_computation.8 | loop fusion | flops 1048576 | bytes 1572864 | tf_op jit(solution)/shard_map/convert_element_type | solution.py:90
  (6 shorter events, 0.1 us)
Async XLA Ops:
  6.5 71.1 %reduce-scatter.2.cloned.1.call-start = ((), (), s32[]{:S(2)}) async-start(), calls=%async_computation.1 | async-start | bytes 2621440 | tf_op jit(solution)/shard_map/reduce_scatter | solution.py:87
  8.1 6.7 %collective-permute-start = (bf16[128,256]{1,0:T(8,128)(2,1)S(1)}, bf16[128,256]{1,0:T(8,128)(2,1)S(1)}, u32[]{:S(2)}, u32[]{:S(2)}) collective-permute-start(bf16[128,256]{1,0:T(8,128)(2,1)S(1)} %constant_dynamic-update-slice_fusion), channel_id=1, source_target_pairs={{0,4},{4,8},{8,12},{12,16},{16,20},{20,24},{24,28},{1,5},{5,9},{9,... | collective-permute-start | bytes 196616 | tf_op jit(solution)/shard_map/ppermute | solution.py:14
  14.8 7.8 %collective-permute-start.1 = (bf16[256,256]{1,0:T(8,128)(2,1)S(1)}, bf16[256,256]{1,0:T(8,128)(2,1)S(1)}, u32[]{:S(2)}, u32[]{:S(2)}) collective-permute-start(bf16[256,256]{1,0:T(8,128)(2,1)S(1)} %pad_maximum_fusion.2), channel_id=1, source_target_pairs={{0,8},{4,12},{8,16},{12,20},{16,24},{20,28},{1,9},{5,13},{9,17},{1... | collective-permute-start | bytes 393224 | tf_op jit(solution)/shard_map/ppermute | solution.py:14
  22.6 9.3 %collective-permute-start.2 = (bf16[512,256]{1,0:T(8,128)(2,1)S(1)}, bf16[512,256]{1,0:T(8,128)(2,1)S(1)}, u32[]{:S(2)}, u32[]{:S(2)}) collective-permute-start(bf16[512,256]{1,0:T(8,128)(2,1)S(1)} %pad_maximum_fusion.1), channel_id=1, source_target_pairs={{0,16},{4,20},{8,24},{12,28},{1,17},{5,21},{9,25},{13,29},{2,18},{... | collective-permute-start | bytes 786440 | tf_op jit(solution)/shard_map/ppermute | solution.py:14
  40.1 37.6 %copy-start = (bf16[128,2048]{1,0:T(8,128)(2,1)S(1)}, bf16[128,2048]{1,0:T(8,128)(2,1)}, u32[]{:S(2)}) copy-start(bf16[128,2048]{1,0:T(8,128)(2,1)} %param.10) | copy-start | bytes 1572868
Sparse Core Ops, SparseCore 0:
  40.2 37.4 reduce-scatter.1
where the time goes:
time: 86.9 us; the launch traced here: 86.5 us
  waiting for transfers between devices  42.8 us (49%)
  starting transfers between devices  15.5 us (18%)
  between operations  13.5 us (16%)
  matrix products  7.13 us (8%)
  local copies, waits for them, and re-layouts  4.07 us (5%)
  other arithmetic  3.51 us (4%)
    reduce_scatter x1, waiting for transfers between devices, local(): lax.psum_scatter(partial_out.astype(jnp.bfloat16), 'head', scatter_dimens...  37.6 us
    ppermute x3, starting transfers between devices, passed_along(): return lax.ppermute(x, axis, pairs)  15.5 us
    dot_general x1, matrix products, local(): jnp.dot(attended, out_weight, preferred_element_type=jnp.float32)  6.03 us
    ppermute x3, waiting for transfers between devices, passed_along(): return lax.ppermute(x, axis, pairs)  5.21 us
    convert_element_type x1, other arithmetic, local(): return (residual.astype(jnp.float32) + summed_out).astype(jnp.bfloat16)  1.96 us
    unnamed x4, local copies, waits for them, and re-layouts  1.79 us
  transfers between devices with their start and end apart: 4, of which 4 were waited for; matrix products, arithmetic and copies ran while one was open for 4% of the time, Pallas kernels for 0%

commit v1 on v0

v1 whole, which is shorter than its diff:
```python
import functools
import math

import jax
import jax.numpy as jnp
from jax import lax
from jax.experimental import pallas as pl
from jax.experimental.pallas import tpu as pltpu
from jax.sharding import PartitionSpec as P

HD = 128
MESH = pl.DeviceIdType.MESH


def each(items, body):
    if len(items) <= 8:
        for item in items:
            body(item)
    elif len(items) > 0:

        @pl.loop(0, len(items))
        def _(step):
            body(items.start + step * items.step)


def kernel(
    dims,
    q_ref,
    k_ref,
    v_ref,
    seg_ref,
    res_hbm,
    w_hbm,
    out_ref,
    kv,
    w,
    tx_pair,
    rx_pair,
    tx_far,
    rx_far,
    acc,
    res,
    kv_send,
    kv_pass,
    kv_recv,
    pair_send,
    pair_recv,
    far_send,
    far_recv,
    w_sem,
    res_sem,
):
    n_ctx, n_head, far, chunks, key_blocks = dims
    rows, q_cols = q_ref.shape
    group = q_cols // HD
    out_cols = out_ref.shape[1]
    width = out_cols // chunks
    pairs = n_head // 2
    me = lax.axis_index("ctx")
    head = lax.axis_index("head")
    side = lax.rem(head, 2)
    pair = lax.div(head, 2)
    mate = head + 1 - 2 * side
    odd = lax.rem(me, 2)
    ctx_mate = me + 1 - 2 * odd

    def pair_at(j):
        return lax.rem(pair + j, pairs)

    order = [j % pairs for j in range(1, pairs + 1)]

    def w_copy(slot, j, other, c):
        part = 2 * pair_at(j) + (1 - side if other else side)
        start = pl.multiple_of(part * out_cols + c * width, 128)
        return pltpu.make_async_copy(
            w_hbm.at[:, pl.ds(start, width)], w.at[slot], w_sem.at[slot]
        )

    w_copies = {}
    for j in order:
        for other in (True, False):
            for c in range(chunks):
                slot = len(w_copies)
                w_copies[j, other, c] = (slot, w_copy(slot, j, other, c))
    for _, copy in w_copies.values():
        copy.start()
    res_copy = pltpu.make_async_copy(res_hbm, res, res_sem)
    res_copy.start()

    barrier = pltpu.get_barrier_semaphore()

    def greet(ctx, hd):
        pl.semaphore_signal(barrier, inc=1, device_id=(ctx, hd), device_id_type=MESH)

    def greet_ctx(k):
        @pl.when(me + k < n_ctx)
        def _():
            greet(me + k, head)

        @pl.when(me - k >= 0)
        def _():
            greet(me - k, head)

    evens = range(2, far + 1, 2)
    each(evens, greet_ctx)
    greet(ctx_mate, head)
    greet(me, mate)
    for j in range(1, pairs):
        greet(me, 2 * pair_at(j) + side)
    kv[0, 0] = k_ref[...]
    kv[0, 1] = v_ref[...]

    def clear(k):
        @pl.when(me - k < 0)
        def _():
            kv[k] = jnp.zeros(kv.shape[1:], kv.dtype)

    each(range(1, far + 1), clear)
    ahead = jnp.minimum(lax.div(n_ctx - 1 - me, 2), far // 2)
    behind = jnp.minimum(lax.div(me, 2), far // 2)
    pl.semaphore_wait(barrier, ahead + behind + 1 + pairs)

    def direct(k):
        return pltpu.make_async_remote_copy(
            src_ref=kv.at[0],
            dst_ref=kv.at[k],
            send_sem=kv_send.at[k],
            recv_sem=kv_recv.at[k],
            device_id=(me + k, head),
            device_id_type=MESH,
        )

    def passed(k, lands):
        return pltpu.make_async_remote_copy(
            src_ref=kv.at[k],
            dst_ref=kv.at[lands],
            send_sem=kv_pass.at[k],
            recv_sem=kv_recv.at[lands],
            device_id=(ctx_mate, head),
            device_id_type=MESH,
        )

    def arrival(k):
        return pltpu.make_async_remote_copy(
            src_ref=kv.at[0],
            dst_ref=kv.at[k],
            send_sem=kv_send.at[k],
            recv_sem=kv_recv.at[k],
            device_id=(ctx_mate, head),
            device_id_type=MESH,
        )

    def send_direct(k):
        @pl.when(me + k < n_ctx)
        def _():
            direct(k).start()

    each(evens, send_direct)

    @pl.when(odd == 0)
    def _():
        passed(0, 1).start()

    def receive_even(k):
        @pl.when(me - k >= 0)
        def _():
            arrival(k).wait_recv()

            @pl.when(odd == 1)
            def _():
                passed(k, k - 1).start()

            @pl.when((odd == 0) & (k < far))
            def _():
                passed(k, jnp.minimum(k + 1, far)).start()

    each(evens, receive_even)

    def receive_odd(k):
        @pl.when(me - k >= 0)
        def _():
            arrival(k).wait_recv()

    each(range(1, far + 1, 2), receive_odd)

    row = lax.broadcasted_iota(jnp.int32, (rows, rows), 0)
    lane = lax.broadcasted_iota(jnp.int32, (rows, rows), 1)
    own_segment = seg_ref[pl.ds(me, 1), :].astype(jnp.float32)
    q_segment = jnp.sum(jnp.where(row == lane, own_segment, 0.0), axis=1, keepdims=True)
    queries = jnp.concatenate([q_ref[:, g * HD : (g + 1) * HD] for g in range(group)], axis=0)
    scale = 1.0 / math.sqrt(HD)

    def attend(step, state):
        best, total, summed = state
        first = step * key_blocks
        visible = []
        for b in range(key_blocks):
            k = first + b
            segment = seg_ref[pl.ds(jnp.maximum(me - k, 0), 1), :].astype(jnp.float32)
            near = (lane - k * rows <= row) & (me - k >= 0)
            visible.append((q_segment == segment) & near)
        visible = jnp.concatenate(
            [jnp.where(v, 0.0, -jnp.inf) for v in visible], axis=1
        )
        visible = jnp.concatenate([visible] * group, axis=0)
        block = kv[pl.ds(first, key_blocks)]
        keys = block[:, 0].reshape(key_blocks * rows, HD)
        values = block[:, 1].reshape(key_blocks * rows, HD)
        scores = lax.dot_general(
            queries, keys, (((1,), (1,)), ((), ())), preferred_element_type=jnp.float32
        )
        scores = scores * scale + visible
        best_new = jnp.maximum(best, jnp.max(scores, axis=1, keepdims=True))
        weights = jnp.exp(scores - best_new)
        shrink = jnp.exp(best - best_new)
        total = total * shrink + jnp.sum(weights, axis=1, keepdims=True)
        summed = summed * shrink + jnp.dot(
            weights.astype(jnp.bfloat16), values, preferred_element_type=jnp.float32
        )
        return best_new, total, summed

    state = (
        jnp.full((group * rows, 1), -1e30, jnp.float32),
        jnp.zeros((group * rows, 1), jnp.float32),
        jnp.zeros((group * rows, HD), jnp.float32),
    )
    steps = (far + 1) // key_blocks
    if steps == 1:
        state = attend(0, state)
    else:
        state = lax.fori_loop(0, steps, attend, state)
    _, total, summed = state
    attended = (summed / total).astype(jnp.bfloat16)
    attended = jnp.concatenate(
        [attended[g * rows : (g + 1) * rows] for g in range(group)], axis=1
    )

    def project(j, other, c):
        slot, copy = w_copies[j, other, c]
        copy.wait()
        return jnp.dot(attended, w[slot], preferred_element_type=jnp.float32)

    def to_mate(i):
        return pltpu.make_async_remote_copy(
            src_ref=tx_pair.at[i],
            dst_ref=rx_pair.at[i],
            send_sem=pair_send.at[i],
            recv_sem=pair_recv.at[i],
            device_id=(me, mate),
            device_id_type=MESH,
        )

    def to_far(j, c):
        i = (j - 1) * chunks + c
        return pltpu.make_async_remote_copy(
            src_ref=tx_far.at[i],
            dst_ref=rx_far.at[i],
            send_sem=far_send.at[i],
            recv_sem=far_recv.at[i],
            device_id=(me, 2 * pair_at(j) + side),
            device_id_type=MESH,
        )

    for j in order:
        for c in range(chunks):
            i = j * chunks + c
            tx_pair[i] = project(j, True, c).astype(jnp.bfloat16)
            to_mate(i).start()
        for c in range(chunks):
            i = j * chunks + c
            mine = project(j, False, c)
            to_mate(i).wait_recv()
            mine = mine + rx_pair[i].astype(jnp.float32)
            if j > 0:
                tx_far[(j - 1) * chunks + c] = mine.astype(jnp.bfloat16)
                to_far(j, c).start()
            else:
                acc[c] = mine
    res_copy.wait()
    for c in range(chunks):
        columns = slice(c * width, (c + 1) * width)
        whole = acc[c] + res[:, columns].astype(jnp.float32)
        for j in range(1, pairs):
            to_far(j, c).wait_recv()
            whole = whole + rx_far[(j - 1) * chunks + c].astype(jnp.float32)
        out_ref[:, columns] = whole.astype(out_ref.dtype)

    for i in range(pairs * chunks):
        to_mate(i).wait_send()
    for j in range(1, pairs):
        for c in range(chunks):
            to_far(j, c).wait_send()

    def sent(k):
        @pl.when(me + k < n_ctx)
        def _():
            direct(k).wait_send()

        @pl.when((me - k >= 0) & ((odd == 1) | (k < far)))
        def _():
            passed(k, k - 1).wait_send()

    each(evens, sent)

    @pl.when(odd == 0)
    def _():
        passed(0, 1).wait_send()


def local(queries, keys, values, segments, residual, out_weight):
    n_ctx, n_head = lax.axis_size("ctx"), lax.axis_size("head")
    rows, out_cols = residual.shape
    depth = out_weight.shape[0]
    far = n_ctx // 2
    pairs = n_head // 2
    width = min(512, out_cols)
    chunks = out_cols // width
    key_blocks = max(b for b in range(1, 9) if (far + 1) % b == 0)
    vmem = pl.BlockSpec(memory_space=pltpu.VMEM)
    hbm = pl.BlockSpec(memory_space=pl.ANY)
    bf16 = jnp.bfloat16
    far_slots = max(1, (pairs - 1) * chunks)
    return pl.pallas_call(
        functools.partial(kernel, (n_ctx, n_head, far, chunks, key_blocks)),
        out_shape=jax.ShapeDtypeStruct((rows, out_cols), bf16),
        in_specs=[vmem, vmem, vmem, vmem, hbm, hbm],
        out_specs=vmem,
        scratch_shapes=[
            pltpu.VMEM((far + 1, 2, rows, HD), bf16),
            pltpu.VMEM((n_head * chunks, depth, width), bf16),
            pltpu.VMEM((pairs * chunks, rows, width), bf16),
            pltpu.VMEM((pairs * chunks, rows, width), bf16),
            pltpu.VMEM((far_slots, rows, width), bf16),
            pltpu.VMEM((far_slots, rows, width), bf16),
            pltpu.VMEM((chunks, rows, width), jnp.float32),
            pltpu.VMEM((rows, out_cols), bf16),
            pltpu.SemaphoreType.DMA((far + 1,)),
            pltpu.SemaphoreType.DMA((far + 1,)),
            pltpu.SemaphoreType.DMA((far + 1,)),
            pltpu.SemaphoreType.DMA((pairs * chunks,)),
            pltpu.SemaphoreType.DMA((pairs * chunks,)),
            pltpu.SemaphoreType.DMA((far_slots,)),
            pltpu.SemaphoreType.DMA((far_slots,)),
            pltpu.SemaphoreType.DMA((n_head * chunks,)),
            pltpu.SemaphoreType.DMA,
        ],
        compiler_params=pltpu.CompilerParams(
            collective_id=0, has_side_effects=True, vmem_limit_bytes=56 * 1024 * 1024
        ),
    )(queries, keys, values, segments.reshape(n_ctx, rows), residual, out_weight)


def solution(mesh):
    placed = (
        P("ctx", "head"),
        P("ctx", "head"),
        P("ctx", "head"),
        P(),
        P("ctx", "head"),
        P("head", None),
    )
    return jax.shard_map(
        local, mesh=mesh, in_specs=placed, out_specs=P("ctx", "head"), check_vma=False
    )
```

time: 86.9 us -> 32.3 us (0.37)
  the two profiles are of different devices: /device:TPU:0 before, /device:TPU:25 now
where the time goes in v1:
time: 32.3 us; the launch traced here: 32.1 us
  Pallas kernels  30.2 us (93%)
  local copies, waits for them, and re-layouts  1.88 us (6%)
    pallas_call x1, Pallas kernels, local(): pl.pallas_call(functools.partial(kernel, (n_ctx, n_head, far, chunks, key...  30.2 us
    unnamed x1, local copies, waits for them, and re-layouts  1.88 us

profile of v1, /device:TPU:25, one launch (start us, length us, event | category | flops | bytes accessed | tf_op | source)
XLA Modules:
  0.0 32.1 jit_solution(8952870870205343511)
XLA Ops:
  0.0 30.2 %shard_map.64 = bf16[128,2048]{1,0:T(8,128)(2,1)} custom-call(bf16[128,512]{1,0:T(8,128)(2,1)} %q_ref.1, bf16[128,128]{1,0:T(8,128)(2,1)} %k_ref.1, bf16[128,128]{1,0:T(8,128)(2,1)} %v_ref.1, s32[8,128]{1,0:T(8,128)} %bitcast.1, bf16[128,2048]{1,0:T(8,128)(2,1)} %res_hbm.1, bf16[512,8192]{1,0:T(8,128)(2,1)} %w_hbm.1), custom_call_target="tpu_custom_call" | custom-call | tf_op jit(solution)/shard_map/pallas_call | solution.py:323
  30.2 1.9 %copy.8 = bf16[128,2048]{1,0:T(8,128)(2,1)} copy(bf16[128,2048]{1,0:T(8,128)(2,1)} %shard_map.64) | data formatting | bytes 1048576

commit v2 on v1

--- a/solution.py
+++ b/solution.py
@@ -23,15 +23,27 @@
             body(items.start + step * items.step)
 
 
+def fold(items, body, state):
+    if len(items) <= 8:
+        for item in items:
+            state = body(item, state)
+        return state
+    return lax.fori_loop(
+        0, len(items), lambda step, s: body(items.start + step * items.step, s), state
+    )
+
+
 def kernel(
     dims,
-    q_ref,
-    k_ref,
-    v_ref,
-    seg_ref,
+    q_hbm,
+    k_hbm,
+    v_hbm,
+    seg_hbm,
     res_hbm,
     w_hbm,
-    out_ref,
+    out_hbm,
+    q_ref,
+    seg_ref,
     kv,
     w,
     tx_pair,
@@ -49,11 +61,13 @@
     far_recv,
     w_sem,
     res_sem,
+    out_sem,
+    in_sem,
 ):
-    n_ctx, n_head, far, chunks, key_blocks = dims
+    n_ctx, n_head, far, chunks = dims
     rows, q_cols = q_ref.shape
     group = q_cols // HD
-    out_cols = out_ref.shape[1]
+    out_cols = out_hbm.shape[1]
     width = out_cols // chunks
     pairs = n_head // 2
     me = lax.axis_index("ctx")
@@ -67,6 +81,40 @@
     def pair_at(j):
         return lax.rem(pair + j, pairs)
 
+    barrier = pltpu.get_barrier_semaphore()
+
+    def greet(ctx, hd):
+        pl.semaphore_signal(barrier, inc=1, device_id=(ctx, hd), device_id_type=MESH)
+
+    def greet_ctx(k):
+        @pl.when(me + k < n_ctx)
+        def _():
+            greet(me + k, head)
+
+        @pl.when(me - k >= 0)
+        def _():
+            greet(me - k, head)
+
+    evens = range(2, far + 1, 2)
+    greet_ctx(2)
+    greet(ctx_mate, head)
+    greet(me, mate)
+    for j in range(1, pairs):
+        greet(me, 2 * pair_at(j) + side)
+    inputs = [
+        pltpu.make_async_copy(source, target, in_sem.at[i])
+        for i, (source, target) in enumerate(
+            [
+                (k_hbm, kv.at[0, 0]),
+                (v_hbm, kv.at[0, 1]),
+                (q_hbm, q_ref),
+                (seg_hbm, seg_ref),
+            ]
+        )
+    ]
+    for copy in inputs:
+        copy.start()
+
     order = [j % pairs for j in range(1, pairs + 1)]
 
     def w_copy(slot, j, other, c):
@@ -78,8 +126,8 @@
 
     w_copies = {}
     for j in order:
-        for other in (True, False):
-            for c in range(chunks):
+        for c in range(chunks):
+            for other in (True, False):
                 slot = len(w_copies)
                 w_copies[j, other, c] = (slot, w_copy(slot, j, other, c))
     for _, copy in w_copies.values():
@@ -87,46 +135,26 @@
     res_copy = pltpu.make_async_copy(res_hbm, res, res_sem)
     res_copy.start()
 
-    barrier = pltpu.get_barrier_semaphore()
-
-    def greet(ctx, hd):
-        pl.semaphore_signal(barrier, inc=1, device_id=(ctx, hd), device_id_type=MESH)
-
-    def greet_ctx(k):
-        @pl.when(me + k < n_ctx)
-        def _():
-            greet(me + k, head)
-
-        @pl.when(me - k >= 0)
-        def _():
-            greet(me - k, head)
-
-    evens = range(2, far + 1, 2)
-    each(evens, greet_ctx)
-    greet(ctx_mate, head)
-    greet(me, mate)
-    for j in range(1, pairs):
-        greet(me, 2 * pair_at(j) + side)
-    kv[0, 0] = k_ref[...]
-    kv[0, 1] = v_ref[...]
-
     def clear(k):
         @pl.when(me - k < 0)
         def _():
             kv[k] = jnp.zeros(kv.shape[1:], kv.dtype)
 
     each(range(1, far + 1), clear)
-    ahead = jnp.minimum(lax.div(n_ctx - 1 - me, 2), far // 2)
-    behind = jnp.minimum(lax.div(me, 2), far // 2)
+    ahead = jnp.where(me + 2 < n_ctx, 1, 0)
+    behind = jnp.where(me - 2 >= 0, 1, 0)
     pl.semaphore_wait(barrier, ahead + behind + 1 + pairs)
+
+    inputs[0].wait()
+    inputs[1].wait()
 
     def direct(k):
         return pltpu.make_async_remote_copy(
-            src_ref=kv.at[0],
+            src_ref=kv.at[k - 2],
             dst_ref=kv.at[k],
             send_sem=kv_send.at[k],
             recv_sem=kv_recv.at[k],
-            device_id=(me + k, head),
+            device_id=(me + 2, head),
             device_id_type=MESH,
         )
 
@@ -150,39 +178,16 @@
             device_id_type=MESH,
         )
 
-    def send_direct(k):
-        @pl.when(me + k < n_ctx)
-        def _():
-            direct(k).start()
-
-    each(evens, send_direct)
+    @pl.when(me + 2 < n_ctx)
+    def _():
+        direct(2).start()
 
     @pl.when(odd == 0)
     def _():
         passed(0, 1).start()
 
-    def receive_even(k):
-        @pl.when(me - k >= 0)
-        def _():
-            arrival(k).wait_recv()
-
-            @pl.when(odd == 1)
-            def _():
-                passed(k, k - 1).start()
-
-            @pl.when((odd == 0) & (k < far))
-            def _():
-                passed(k, jnp.minimum(k + 1, far)).start()
-
-    each(evens, receive_even)
-
-    def receive_odd(k):
-        @pl.when(me - k >= 0)
-        def _():
-            arrival(k).wait_recv()
-
-    each(range(1, far + 1, 2), receive_odd)
-
+    inputs[2].wait()
+    inputs[3].wait()
     row = lax.broadcasted_iota(jnp.int32, (rows, rows), 0)
     lane = lax.broadcasted_iota(jnp.int32, (rows, rows), 1)
     own_segment = seg_ref[pl.ds(me, 1), :].astype(jnp.float32)
@@ -190,22 +195,14 @@
     queries = jnp.concatenate([q_ref[:, g * HD : (g + 1) * HD] for g in range(group)], axis=0)
     scale = 1.0 / math.sqrt(HD)
 
-    def attend(step, state):
+    def attend(k, state):
         best, total, summed = state
-        first = step * key_blocks
-        visible = []
-        for b in range(key_blocks):
-            k = first + b
-            segment = seg_ref[pl.ds(jnp.maximum(me - k, 0), 1), :].astype(jnp.float32)
-            near = (lane - k * rows <= row) & (me - k >= 0)
-            visible.append((q_segment == segment) & near)
-        visible = jnp.concatenate(
-            [jnp.where(v, 0.0, -jnp.inf) for v in visible], axis=1
-        )
+        segment = seg_ref[pl.ds(jnp.maximum(me - k, 0), 1), :].astype(jnp.float32)
+        near = (lane - k * rows <= row) & (me - k >= 0)
+        visible = jnp.where((q_segment == segment) & near, 0.0, -jnp.inf)
         visible = jnp.concatenate([visible] * group, axis=0)
-        block = kv[pl.ds(first, key_blocks)]
-        keys = block[:, 0].reshape(key_blocks * rows, HD)
-        values = block[:, 1].reshape(key_blocks * rows, HD)
+        keys = kv[k, 0]
+        values = kv[k, 1]
         scores = lax.dot_general(
             queries, keys, (((1,), (1,)), ((), ())), preferred_element_type=jnp.float32
         )
@@ -224,11 +221,36 @@
         jnp.zeros((group * rows, 1), jnp.float32),
         jnp.zeros((group * rows, HD), jnp.float32),
     )
-    steps = (far + 1) // key_blocks
-    if steps == 1:
-        state = attend(0, state)
-    else:
-        state = lax.fori_loop(0, steps, attend, state)
+    state = attend(0, state)
+
+    def take_even(k, state):
+        @pl.when(me - k >= 0)
+        def _():
+            arrival(k).wait_recv()
+
+            @pl.when((me + 2 < n_ctx) & (k < far))
+            def _():
+                direct(jnp.minimum(k + 2, far)).start()
+
+            @pl.when(odd == 1)
+            def _():
+                passed(k, k - 1).start()
+
+            @pl.when((odd == 0) & (k < far))
+            def _():
+                passed(k, jnp.minimum(k + 1, far)).start()
+
+        return attend(k, state)
+
+    def take_odd(k, state):
+        @pl.when(me - k >= 0)
+        def _():
+            arrival(k).wait_recv()
+
+        return attend(k, state)
+
+    state = fold(evens, take_even, state)
+    state = fold(range(1, far + 1, 2), take_odd, state)
     _, total, summed = state
     attended = (summed / total).astype(jnp.bfloat16)
     attended = jnp.concatenate(
@@ -261,12 +283,16 @@
             device_id_type=MESH,
         )
 
+    lag = min(2, chunks)
     for j in order:
-        for c in range(chunks):
-            i = j * chunks + c
-            tx_pair[i] = project(j, True, c).astype(jnp.bfloat16)
-            to_mate(i).start()
-        for c in range(chunks):
+        for t in range(chunks + lag):
+            if t < chunks:
+                i = j * chunks + t
+                tx_pair[i] = project(j, True, t).astype(jnp.bfloat16)
+                to_mate(i).start()
+            if t < lag:
+                continue
+            c = t - lag
             i = j * chunks + c
             mine = project(j, False, c)
             to_mate(i).wait_recv()
@@ -277,14 +303,23 @@
             else:
                 acc[c] = mine
     res_copy.wait()
+    out_copies = []
     for c in range(chunks):
         columns = slice(c * width, (c + 1) * width)
         whole = acc[c] + res[:, columns].astype(jnp.float32)
         for j in range(1, pairs):
             to_far(j, c).wait_recv()
             whole = whole + rx_far[(j - 1) * chunks + c].astype(jnp.float32)
-        out_ref[:, columns] = whole.astype(out_ref.dtype)
-
+        res[:, columns] = whole.astype(res.dtype)
+        out_copies.append(
+            pltpu.make_async_copy(
+                res.at[:, columns], out_hbm.at[:, columns], out_sem.at[c]
+            )
+        )
+        out_copies[c].start()
+
+    for copy in out_copies:
+        copy.wait()
     for i in range(pairs * chunks):
         to_mate(i).wait_send()
     for j in range(1, pairs):
@@ -292,7 +327,7 @@
             to_far(j, c).wait_send()
 
     def sent(k):
-        @pl.when(me + k < n_ctx)
+        @pl.when((me + 2 < n_ctx) & (me - (k - 2) >= 0))
         def _():
             direct(k).wait_send()
 
@@ -315,17 +350,17 @@
     pairs = n_head // 2
     width = min(512, out_cols)
     chunks = out_cols // width
-    key_blocks = max(b for b in range(1, 9) if (far + 1) % b == 0)
-    vmem = pl.BlockSpec(memory_space=pltpu.VMEM)
     hbm = pl.BlockSpec(memory_space=pl.ANY)
     bf16 = jnp.bfloat16
     far_slots = max(1, (pairs - 1) * chunks)
     return pl.pallas_call(
-        functools.partial(kernel, (n_ctx, n_head, far, chunks, key_blocks)),
+        functools.partial(kernel, (n_ctx, n_head, far, chunks)),
         out_shape=jax.ShapeDtypeStruct((rows, out_cols), bf16),
-        in_specs=[vmem, vmem, vmem, vmem, hbm, hbm],
-        out_specs=vmem,
+        in_specs=[hbm] * 6,
+        out_specs=hbm,
         scratch_shapes=[
+            pltpu.VMEM(queries.shape, bf16),
+            pltpu.VMEM((n_ctx, rows), jnp.int32),
             pltpu.VMEM((far + 1, 2, rows, HD), bf16),
             pltpu.VMEM((n_head * chunks, depth, width), bf16),
             pltpu.VMEM((pairs * chunks, rows, width), bf16),
@@ -343,6 +378,8 @@
             pltpu.SemaphoreType.DMA((far_slots,)),
             pltpu.SemaphoreType.DMA((n_head * chunks,)),
             pltpu.SemaphoreType.DMA,
+            pltpu.SemaphoreType.DMA((chunks,)),
+            pltpu.SemaphoreType.DMA((4,)),
         ],
         compiler_params=pltpu.CompilerParams(
             collective_id=0, has_side_effects=True, vmem_limit_bytes=56 * 1024 * 1024

time: 32.3 us -> 31.1 us (0.963)
  Pallas kernels: 30.2 us -> 29.1 us
    pallas_call x1, Pallas kernels: 30.2 us -> 29.1 us  [local(): pl.pallas_call(functools.partial(kernel, (n_ctx, n_head, far, chunks)), o...]
where the time goes in v2:
time: 31.1 us; the launch traced here: 31 us
  Pallas kernels  29.1 us (94%)
  local copies, waits for them, and re-layouts  1.88 us (6%)
    pallas_call x1, Pallas kernels, local(): pl.pallas_call(functools.partial(kernel, (n_ctx, n_head, far, chunks)), o...  29.1 us
    unnamed x1, local copies, waits for them, and re-layouts  1.88 us

profile of v2, /device:TPU:25, one launch (start us, length us, event | category | flops | bytes accessed | tf_op | source)
XLA Modules:
  0.0 31.0 jit_solution(8949397527364041227)
XLA Ops:
  0.0 29.1 %shard_map.64 = bf16[128,2048]{1,0:T(8,128)(2,1)} custom-call(bf16[128,512]{1,0:T(8,128)(2,1)} %q_hbm.1, bf16[128,128]{1,0:T(8,128)(2,1)} %k_hbm.1, bf16[128,128]{1,0:T(8,128)(2,1)} %v_hbm.1, s32[8,128]{1,0:T(8,128)} %bitcast.1, bf16[128,2048]{1,0:T(8,128)(2,1)} %res_hbm.1, bf16[512,8192]{1,0:T(8,128)(2,1)} %w_hbm.1), custom_call_target="tpu_custom_call" | custom-call | tf_op jit(solution)/shard_map/pallas_call | solution.py:356
  29.1 1.9 %copy.8 = bf16[128,2048]{1,0:T(8,128)(2,1)} copy(bf16[128,2048]{1,0:T(8,128)(2,1)} %shard_map.64) | data formatting | bytes 1048576

commit v3 on v2

--- a/solution.py
+++ b/solution.py
@@ -130,10 +130,7 @@
             for other in (True, False):
                 slot = len(w_copies)
                 w_copies[j, other, c] = (slot, w_copy(slot, j, other, c))
-    for _, copy in w_copies.values():
-        copy.start()
     res_copy = pltpu.make_async_copy(res_hbm, res, res_sem)
-    res_copy.start()
 
     def clear(k):
         @pl.when(me - k < 0)
@@ -148,43 +145,52 @@
     inputs[0].wait()
     inputs[1].wait()
 
-    def direct(k):
+    def direct_part(p, k):
         return pltpu.make_async_remote_copy(
-            src_ref=kv.at[k - 2],
-            dst_ref=kv.at[k],
-            send_sem=kv_send.at[k],
-            recv_sem=kv_recv.at[k],
+            src_ref=kv.at[k - 2, p],
+            dst_ref=kv.at[k, p],
+            send_sem=kv_send.at[k, p],
+            recv_sem=kv_recv.at[k, p],
             device_id=(me + 2, head),
             device_id_type=MESH,
         )
 
-    def passed(k, lands):
+    def passed_part(p, k, lands):
         return pltpu.make_async_remote_copy(
-            src_ref=kv.at[k],
-            dst_ref=kv.at[lands],
-            send_sem=kv_pass.at[k],
-            recv_sem=kv_recv.at[lands],
+            src_ref=kv.at[k, p],
+            dst_ref=kv.at[lands, p],
+            send_sem=kv_pass.at[k, p],
+            recv_sem=kv_recv.at[lands, p],
             device_id=(ctx_mate, head),
             device_id_type=MESH,
         )
 
-    def arrival(k):
+    def arrival_part(p, k):
         return pltpu.make_async_remote_copy(
-            src_ref=kv.at[0],
-            dst_ref=kv.at[k],
-            send_sem=kv_send.at[k],
-            recv_sem=kv_recv.at[k],
+            src_ref=kv.at[0, p],
+            dst_ref=kv.at[k, p],
+            send_sem=kv_send.at[k, p],
+            recv_sem=kv_recv.at[k, p],
             device_id=(ctx_mate, head),
             device_id_type=MESH,
         )
 
+    def both(make, *args):
+        return [make(p, *args) for p in range(2)]
+
     @pl.when(me + 2 < n_ctx)
     def _():
-        direct(2).start()
+        for copy in both(direct_part, 2):
+            copy.start()
 
     @pl.when(odd == 0)
     def _():
-        passed(0, 1).start()
+        for copy in both(passed_part, 0, 1):
+            copy.start()
+
+    for _, copy in w_copies.values():
+        copy.start()
+    res_copy.start()
 
     inputs[2].wait()
     inputs[3].wait()
@@ -226,26 +232,28 @@
     def take_even(k, state):
         @pl.when(me - k >= 0)
         def _():
-            arrival(k).wait_recv()
-
-            @pl.when((me + 2 < n_ctx) & (k < far))
-            def _():
-                direct(jnp.minimum(k + 2, far)).start()
-
-            @pl.when(odd == 1)
-            def _():
-                passed(k, k - 1).start()
-
-            @pl.when((odd == 0) & (k < far))
-            def _():
-                passed(k, jnp.minimum(k + 1, far)).start()
+            for p in range(2):
+                arrival_part(p, k).wait_recv()
+
+                @pl.when((me + 2 < n_ctx) & (k < far))
+                def _():
+                    direct_part(p, jnp.minimum(k + 2, far)).start()
+
+                @pl.when(odd == 1)
+                def _():
+                    passed_part(p, k, k - 1).start()
+
+                @pl.when((odd == 0) & (k < far))
+                def _():
+                    passed_part(p, k, jnp.minimum(k + 1, far)).start()
 
         return attend(k, state)
 
     def take_odd(k, state):
         @pl.when(me - k >= 0)
         def _():
-            arrival(k).wait_recv()
+            for copy in both(arrival_part, k):
+                copy.wait_recv()
 
         return attend(k, state)
 
@@ -329,17 +337,20 @@
     def sent(k):
         @pl.when((me + 2 < n_ctx) & (me - (k - 2) >= 0))
         def _():
-            direct(k).wait_send()
+            for copy in both(direct_part, k):
+                copy.wait_send()
 
         @pl.when((me - k >= 0) & ((odd == 1) | (k < far)))
         def _():
-            passed(k, k - 1).wait_send()
+            for copy in both(passed_part, k, k - 1):
+                copy.wait_send()
 
     each(evens, sent)
 
     @pl.when(odd == 0)
     def _():
-        passed(0, 1).wait_send()
+        for copy in both(passed_part, 0, 1):
+            copy.wait_send()
 
 
 def local(queries, keys, values, segments, residual, out_weight):
@@ -369,9 +380,9 @@
             pltpu.VMEM((far_slots, rows, width), bf16),
             pltpu.VMEM((chunks, rows, width), jnp.float32),
             pltpu.VMEM((rows, out_cols), bf16),
-            pltpu.SemaphoreType.DMA((far + 1,)),
-            pltpu.SemaphoreType.DMA((far + 1,)),
-            pltpu.SemaphoreType.DMA((far + 1,)),
+            pltpu.SemaphoreType.DMA((far + 1, 2)),
+            pltpu.SemaphoreType.DMA((far + 1, 2)),
+            pltpu.SemaphoreType.DMA((far + 1, 2)),
             pltpu.SemaphoreType.DMA((pairs * chunks,)),
             pltpu.SemaphoreType.DMA((pairs * chunks,)),
             pltpu.SemaphoreType.DMA((far_slots,)),

time: 31.1 us -> 29.6 us (0.952)
  Pallas kernels: 29.1 us -> 27.6 us
    pallas_call x1, Pallas kernels: 29.1 us -> 27.6 us  [local(): pl.pallas_call(functools.partial(kernel, (n_ctx, n_head, far, chunks)), o...]
where the time goes in v3:
time: 29.6 us; the launch traced here: 29.5 us
  Pallas kernels  27.6 us (93%)
  local copies, waits for them, and re-layouts  1.88 us (6%)
    pallas_call x1, Pallas kernels, local(): pl.pallas_call(functools.partial(kernel, (n_ctx, n_head, far, chunks)), o...  27.6 us
    unnamed x1, local copies, waits for them, and re-layouts  1.88 us

profile of v3, /device:TPU:25, one launch (start us, length us, event | category | flops | bytes accessed | tf_op | source)
XLA Modules:
  0.0 29.5 jit_solution(6603883062291638097)
XLA Ops:
  0.0 27.6 %shard_map.64 = bf16[128,2048]{1,0:T(8,128)(2,1)} custom-call(bf16[128,512]{1,0:T(8,128)(2,1)} %q_hbm.1, bf16[128,128]{1,0:T(8,128)(2,1)} %k_hbm.1, bf16[128,128]{1,0:T(8,128)(2,1)} %v_hbm.1, s32[8,128]{1,0:T(8,128)} %bitcast.1, bf16[128,2048]{1,0:T(8,128)(2,1)} %res_hbm.1, bf16[512,8192]{1,0:T(8,128)(2,1)} %w_hbm.1), custom_call_target="tpu_custom_call" | custom-call | tf_op jit(solution)/shard_map/pallas_call | solution.py:367
  27.6 1.9 %copy.8 = bf16[128,2048]{1,0:T(8,128)(2,1)} copy(bf16[128,2048]{1,0:T(8,128)(2,1)} %shard_map.64) | data formatting | bytes 1048576

commit v4 on v3

--- a/solution.py
+++ b/solution.py
@@ -257,8 +257,7 @@
 
         return attend(k, state)
 
-    state = fold(evens, take_even, state)
-    state = fold(range(1, far + 1, 2), take_odd, state)
+    state = fold(evens, lambda k, s: take_odd(k - 1, take_even(k, s)), state)
     _, total, summed = state
     attended = (summed / total).astype(jnp.bfloat16)
     attended = jnp.concatenate(
@@ -291,7 +290,7 @@
             device_id_type=MESH,
         )
 
-    lag = min(2, chunks)
+    lag = min(1, chunks)
     for j in order:
         for t in range(chunks + lag):
             if t < chunks:

time: 29.6 us -> 29.3 us (0.990)
  Pallas kernels: 27.6 us -> 27.2 us
    pallas_call x1, Pallas kernels: 27.6 us -> 27.2 us  [local(): pl.pallas_call(functools.partial(kernel, (n_ctx, n_head, far, chunks)), o...]
where the time goes in v4:
time: 29.3 us; the launch traced here: 29.1 us
  Pallas kernels  27.2 us (93%)
  local copies, waits for them, and re-layouts  1.88 us (6%)
    pallas_call x1, Pallas kernels, local(): pl.pallas_call(functools.partial(kernel, (n_ctx, n_head, far, chunks)), o...  27.2 us
    unnamed x1, local copies, waits for them, and re-layouts  1.88 us

profile of v4, /device:TPU:25, one launch (start us, length us, event | category | flops | bytes accessed | tf_op | source)
XLA Modules:
  0.0 29.1 jit_solution(6674458918738064770)
XLA Ops:
  0.0 27.2 %shard_map.64 = bf16[128,2048]{1,0:T(8,128)(2,1)} custom-call(bf16[128,512]{1,0:T(8,128)(2,1)} %q_hbm.1, bf16[128,128]{1,0:T(8,128)(2,1)} %k_hbm.1, bf16[128,128]{1,0:T(8,128)(2,1)} %v_hbm.1, s32[8,128]{1,0:T(8,128)} %bitcast.1, bf16[128,2048]{1,0:T(8,128)(2,1)} %res_hbm.1, bf16[512,8192]{1,0:T(8,128)(2,1)} %w_hbm.1), custom_call_target="tpu_custom_call" | custom-call | tf_op jit(solution)/shard_map/pallas_call | solution.py:366
  27.2 1.9 %copy.8 = bf16[128,2048]{1,0:T(8,128)(2,1)} copy(bf16[128,2048]{1,0:T(8,128)(2,1)} %shard_map.64) | data formatting | bytes 1048576

commit v5 on v4

--- a/solution.py
+++ b/solution.py
@@ -105,8 +105,10 @@
         pltpu.make_async_copy(source, target, in_sem.at[i])
         for i, (source, target) in enumerate(
             [
-                (k_hbm, kv.at[0, 0]),
-                (v_hbm, kv.at[0, 1]),
+                (k_hbm.at[: rows // 2], kv.at[0, 0]),
+                (k_hbm.at[rows // 2 :], kv.at[0, 1]),
+                (v_hbm.at[: rows // 2], kv.at[0, 2]),
+                (v_hbm.at[rows // 2 :], kv.at[0, 3]),
                 (q_hbm, q_ref),
                 (seg_hbm, seg_ref),
             ]
@@ -142,8 +144,8 @@
     behind = jnp.where(me - 2 >= 0, 1, 0)
     pl.semaphore_wait(barrier, ahead + behind + 1 + pairs)
 
-    inputs[0].wait()
-    inputs[1].wait()
+    for copy in inputs[:4]:
+        copy.wait()
 
     def direct_part(p, k):
         return pltpu.make_async_remote_copy(
@@ -176,7 +178,7 @@
         )
 
     def both(make, *args):
-        return [make(p, *args) for p in range(2)]
+        return [make(p, *args) for p in range(4)]
 
     @pl.when(me + 2 < n_ctx)
     def _():
@@ -192,8 +194,8 @@
         copy.start()
     res_copy.start()
 
-    inputs[2].wait()
-    inputs[3].wait()
+    inputs[4].wait()
+    inputs[5].wait()
     row = lax.broadcasted_iota(jnp.int32, (rows, rows), 0)
     lane = lax.broadcasted_iota(jnp.int32, (rows, rows), 1)
     own_segment = seg_ref[pl.ds(me, 1), :].astype(jnp.float32)
@@ -207,8 +209,8 @@
         near = (lane - k * rows <= row) & (me - k >= 0)
         visible = jnp.where((q_segment == segment) & near, 0.0, -jnp.inf)
         visible = jnp.concatenate([visible] * group, axis=0)
-        keys = kv[k, 0]
-        values = kv[k, 1]
+        keys = kv[k, :2].reshape(rows, HD)
+        values = kv[k, 2:].reshape(rows, HD)
         scores = lax.dot_general(
             queries, keys, (((1,), (1,)), ((), ())), preferred_element_type=jnp.float32
         )
@@ -232,7 +234,7 @@
     def take_even(k, state):
         @pl.when(me - k >= 0)
         def _():
-            for p in range(2):
+            for p in range(4):
                 arrival_part(p, k).wait_recv()
 
                 @pl.when((me + 2 < n_ctx) & (k < far))
@@ -371,7 +373,7 @@
         scratch_shapes=[
             pltpu.VMEM(queries.shape, bf16),
             pltpu.VMEM((n_ctx, rows), jnp.int32),
-            pltpu.VMEM((far + 1, 2, rows, HD), bf16),
+            pltpu.VMEM((far + 1, 4, rows // 2, HD), bf16),
             pltpu.VMEM((n_head * chunks, depth, width), bf16),
             pltpu.VMEM((pairs * chunks, rows, width), bf16),
             pltpu.VMEM((pairs * chunks, rows, width), bf16),
@@ -379,9 +381,9 @@
             pltpu.VMEM((far_slots, rows, width), bf16),
             pltpu.VMEM((chunks, rows, width), jnp.float32),
             pltpu.VMEM((rows, out_cols), bf16),
-            pltpu.SemaphoreType.DMA((far + 1, 2)),
-            pltpu.SemaphoreType.DMA((far + 1, 2)),
-            pltpu.SemaphoreType.DMA((far + 1, 2)),
+            pltpu.SemaphoreType.DMA((far + 1, 4)),
+            pltpu.SemaphoreType.DMA((far + 1, 4)),
+            pltpu.SemaphoreType.DMA((far + 1, 4)),
             pltpu.SemaphoreType.DMA((pairs * chunks,)),
             pltpu.SemaphoreType.DMA((pairs * chunks,)),
             pltpu.SemaphoreType.DMA((far_slots,)),
@@ -389,7 +391,7 @@
             pltpu.SemaphoreType.DMA((n_head * chunks,)),
             pltpu.SemaphoreType.DMA,
             pltpu.SemaphoreType.DMA((chunks,)),
-            pltpu.SemaphoreType.DMA((4,)),
+            pltpu.SemaphoreType.DMA((6,)),
         ],
         compiler_params=pltpu.CompilerParams(
             collective_id=0, has_side_effects=True, vmem_limit_bytes=56 * 1024 * 1024

time: 29.3 us -> 29.4 us (level)
  no operation moved by 1% of the time
where the time goes in v5:
time: 29.4 us; the launch traced here: 29.2 us
  Pallas kernels  27.3 us (93%)
  local copies, waits for them, and re-layouts  1.88 us (6%)
    pallas_call x1, Pallas kernels, local(): pl.pallas_call(functools.partial(kernel, (n_ctx, n_head, far, chunks)), o...  27.3 us
    unnamed x1, local copies, waits for them, and re-layouts  1.88 us

profile of v5, /device:TPU:25, one launch (start us, length us, event | category | flops | bytes accessed | tf_op | source)
XLA Modules:
  0.0 29.2 jit_solution(4870442019390592773)
XLA Ops:
  0.0 27.3 %shard_map.64 = bf16[128,2048]{1,0:T(8,128)(2,1)} custom-call(bf16[128,512]{1,0:T(8,128)(2,1)} %q_hbm.1, bf16[128,128]{1,0:T(8,128)(2,1)} %k_hbm.1, bf16[128,128]{1,0:T(8,128)(2,1)} %v_hbm.1, s32[8,128]{1,0:T(8,128)} %bitcast.1, bf16[128,2048]{1,0:T(8,128)(2,1)} %res_hbm.1, bf16[512,8192]{1,0:T(8,128)(2,1)} %w_hbm.1), custom_call_target="tpu_custom_call" | custom-call | tf_op jit(solution)/shard_map/pallas_call | solution.py:368
  27.3 1.9 %copy.8 = bf16[128,2048]{1,0:T(8,128)(2,1)} copy(bf16[128,2048]{1,0:T(8,128)(2,1)} %shard_map.64) | data formatting | bytes 1048576
